TPU v7x, 768 devices: a whole 4x8x12 slice. The times are simulated.
768 devices in a mesh: row: 96 (over z, x, y_hi), col: 8 (over y_lo, core).
Axes of the slice: x: 4, y: 8 (y_hi: 2, y_lo: 4; y = y_hi * 4 + y_lo), z: 12, core: 2. Of those that a mesh axis runs over, the one named last changes fastest.
Arguments:
- vectors: float32 [393216, 16], P(('row', 'col')), may hold values from -6 to 6
- tiles: float32 [96, 8, 256, 64, 64], P('row', 'col'), may hold values from -0.125 to 0.125
- tile_rows: int32 [96, 8, 256], P('row', 'col'), may hold values from 0 to 63
- tile_cols: int32 [96, 8, 256], P('row', 'col'), may hold values from 0 to 767
- tile_count: int32 [96, 8], P('row', 'col'), may hold values from 1 to 256, as said below
Outputs:
- product: float32 [393216, 16], P(('row', 'col'))
Inputs may be any that keep to these rules, and one draw needn't show every extreme that they name: `tile_count`: device (0, c) has all 256 slots live; devices further along row hold fewer.
All inputs are finite; a program needn't handle non-finite values.
Results may differ from a plain program's by a relative error of at most 0.0001.
Values sent between devices are 32-bit elements; how exact they have to be, the bound alone decides.
No kernel may reach another device: no remote copies, remote signals or barrier semaphores. Data moves between devices by JAX's collectives and lax.ppermute only.
A program may use at most 64 MiB of HBM per device.

v0:
```python
import jax
import jax.numpy as jnp
from jax import lax
from jax.experimental import pallas as pl
from jax.experimental.pallas import tpu as pltpu
from jax.sharding import PartitionSpec as P

VEC = 16
TILE = 64
TPD = 256
S = 512
RT = 64
CT = 768
NZ, NX, NY = 12, 4, 2
NCOL = 8
PT = S // TILE
WIDE = VEC * TILE
CHUNK = CT // NX
GROUP = 4
LANES = 128
CHUNKS = 7
BACK_MIB, FORTH_MIB = 58, 48


def row_index(z, x, y):
    return ((z % NZ) * NX + (x % NX)) * NY + (y % NY)


def row_shift(dx=0, dy=0):
    return [
        (row_index(z, x, y), row_index(z, x + dx, y + dy))
        for z in range(NZ)
        for x in range(NX)
        for y in range(NY)
    ]


Z_GROUPS = [[row_index(z, x, y) for z in range(NZ)] for x in range(NX) for y in range(NY)]
XY_GROUPS = [[row_index(z, x, y) for x in range(NX) for y in range(NY)] for z in range(NZ)]
RING_GROUPS = [
    [row_index(z, x, y) * NCOL + c for y in range(NY) for c in range(NCOL)]
    for z in range(NZ)
    for x in range(NX)
]


def three_parts(value):
    first = value.astype(jnp.bfloat16)
    rest = value - first.astype(jnp.float32)
    second = rest.astype(jnp.bfloat16)
    third = (rest - second.astype(jnp.float32)).astype(jnp.bfloat16)
    return first, second, third


def indicator(condition):
    return jnp.where(condition, 1.0, 0.0).astype(jnp.bfloat16)


def iota(shape, dim):
    return lax.broadcasted_iota(jnp.int32, shape, dim)


def put(halves, value):
    for half in range(TPD // LANES):
        halves[half] = value[:, half * LANES : (half + 1) * LANES]


def whole(halves):
    return jnp.concatenate([halves[half] for half in range(TPD // LANES)], axis=1)


def column(row):
    return jnp.broadcast_to(row, (8, row.shape[1])).T[:, :1]


def fetch(pairs, arrived):
    copies = [pltpu.make_async_copy(*pair, arrived.at[i]) for i, pair in enumerate(pairs)]
    for copy in copies:
        copy.start()
    return copies


def pick(picked, onehot, value):
    dims = (((0,), (0,)), ((), ()))
    put(
        picked,
        lax.dot_general(
            jnp.concatenate(three_parts(value)),
            jnp.concatenate([onehot] * 3),
            dims,
            preferred_element_type=jnp.float32,
        ),
    )


def place(onehot, value):
    return lax.dot_general(
        jnp.concatenate([onehot] * 3, axis=1),
        jnp.concatenate(three_parts(value), axis=1),
        (((1,), (1,)), ((), ())),
        preferred_element_type=jnp.float32,
    )


def backward_kernel(
    count, row, col, rows, rids_far, cids_far, far, out, pair, side, rids, cids, tiles, arrived, picked, summed
):
    own = rows.at[pl.ds(pl.multiple_of((row[0, 0] & 1) * RT, RT), RT)]
    pairs = [(own, side), (rids_far, rids), (cids_far, cids), (far, tiles)]
    for y in range(NY):
        piece = rows.at[pl.ds(pl.multiple_of(y * RT + col[0, 0] * PT, PT), PT)]
        pairs.append((piece, pair.at[pl.ds(y * PT, PT)]))
    copies = fetch(pairs, arrived)
    for copy in copies[:3]:
        copy.wait()
    pick(picked, indicator(iota((RT, TPD), 0) == rids[...]), side[...])
    live = iota((1, TPD), 1) < count[0, 0]
    at_col = indicator((iota((CT, TPD), 0) == cids[...]) & live)
    copies[3].wait()
    for group in range(VEC // GROUP):
        for half in range(TPD // LANES):
            lanes = pl.ds(half * LANES, LANES)

            def step(a, totals):
                tile = tiles[a, :, lanes]
                return tuple(
                    total + tile * picked[half, pl.ds((group * GROUP + v) * TILE + a, 1), :]
                    for v, total in enumerate(totals)
                )

            zero = jnp.zeros((TILE, LANES), jnp.float32)
            totals = lax.fori_loop(0, TILE, step, (zero,) * GROUP, unroll=64)
            for v, total in enumerate(totals):
                summed[half, v * TILE : (v + 1) * TILE, :] = total
        out[:, group * GROUP * TILE : (group + 1) * GROUP * TILE] = place(at_col, whole(summed))
    for copy in copies[4:]:
        copy.wait()


def forward_kernel(count, row, *refs):
    chunks, refs = refs[:CHUNKS], refs[CHUNKS:]
    cids_far, rids_far, far, out, cids, rids, tiles, arrived, picked, summed = refs
    copies = fetch([(cids_far, cids), (rids_far, rids), (far, tiles)], arrived)
    for copy in copies[:2]:
        copy.wait()
    tile = cids[...]
    x, rest = (tile >> 4) & 3, (tile >> 6) * (NY * PT) + (tile & 15)
    places = (((row[0, 0] >> 1) - x) & 3) * CHUNK + rest
    side = jnp.concatenate([chunk[...] for chunk in chunks])
    pick(picked, indicator(iota((CT, TPD), 0) == places), side)
    live = iota((1, TPD), 1) < count[0, 0]
    at_row = indicator((iota((RT, TPD), 0) == rids[...]) & live)
    copies[2].wait()
    for group in range(VEC // GROUP):
        for half in range(TPD // LANES):
            lanes = pl.ds(half * LANES, LANES)
            blocks = [
                picked[half, (group * GROUP + v) * TILE : (group * GROUP + v + 1) * TILE, :]
                for v in range(GROUP)
            ]

            def step(a, carry):
                tile = tiles[a, :, lanes]
                for v, block in enumerate(blocks):
                    summed[half, pl.ds(v * TILE + a, 1), :] = jnp.sum(
                        tile * block, axis=0, keepdims=True
                    )
                return carry

            lax.fori_loop(0, TILE, step, 0, unroll=64)
        out[:, group * GROUP * TILE : (group + 1) * GROUP * TILE] = place(at_row, whole(summed))


def run(kernel, outs, vmem_mib, scratch, scalars, near, far):
    in_vmem, in_hbm = (pl.BlockSpec(memory_space=space) for space in (pltpu.VMEM, pltpu.HBM))
    return pl.pallas_call(
        kernel,
        out_shape=[jax.ShapeDtypeStruct((rows, WIDE), jnp.float32) for rows in outs],
        in_specs=[pl.BlockSpec(memory_space=pltpu.SMEM)] * len(scalars)
        + [in_vmem] * len(near)
        + [in_hbm] * len(far),
        out_specs=[in_vmem] + [in_hbm] * (len(outs) - 1),
        scratch_shapes=scratch
        + [
            pltpu.VMEM((1, TPD), jnp.int32),
            pltpu.VMEM((1, TPD), jnp.int32),
            pltpu.VMEM((TILE, TILE, TPD), jnp.float32),
            pltpu.SemaphoreType.DMA((6,)),
            pltpu.VMEM((TPD // LANES, WIDE, LANES), jnp.float32),
            pltpu.VMEM((TPD // LANES, GROUP * TILE, LANES), jnp.float32),
        ],
        compiler_params=pltpu.CompilerParams(vmem_limit_bytes=vmem_mib * 1024 * 1024),
        cost_estimate=pl.CostEstimate(
            flops=10_000_000_000, bytes_accessed=8 * 1024 * 1024, transcendentals=0
        ),
    )(*scalars, *near, *far)


def local(vectors, tiles, tile_rows, tile_cols, tile_count):
    me, me_col = lax.axis_index("row"), lax.axis_index("col")
    piece = vectors.T.reshape(VEC, PT, TILE).transpose(1, 0, 2).reshape(PT, WIDE)
    block = tiles[0, 0].transpose(1, 2, 0)
    rids, cids = tile_rows[0], tile_cols[0]

    rows = lax.all_gather(
        piece, ("row", "col"), axis_index_groups=RING_GROUPS, axis=0, tiled=True
    )
    col_part, pair = run(
        backward_kernel,
        [CT, NY * PT],
        BACK_MIB,
        [pltpu.VMEM((RT, WIDE), jnp.float32)],
        (tile_count, me.reshape(1, 1), me_col.reshape(1, 1)),
        (),
        (rows, rids, cids, block),
    )
    col_sum = lax.psum_scatter(
        col_part, "row", axis_index_groups=Z_GROUPS, scatter_dimension=0, tiled=True
    )

    mine = lax.all_gather(
        pair,
        "row",
        axis_index_groups=Z_GROUPS,
        axis=0,
        tiled=True,
    )
    first, second = mine[: CHUNK // 2], mine[CHUNK // 2 :]
    left_first = lax.ppermute(first, "row", row_shift(dx=1))
    right_second = lax.ppermute(second, "row", row_shift(dx=-1))
    left_second = lax.ppermute(second, "row", row_shift(dx=1))
    right_first = lax.ppermute(first, "row", row_shift(dx=-1))
    far_first = lax.ppermute(left_first, "row", row_shift(dx=1))
    far_second = lax.ppermute(right_second, "row", row_shift(dx=-1))
    chunks = [mine, left_first, left_second, far_first, far_second, right_first, right_second]
    me_too, col_sum = lax.optimization_barrier((me.reshape(1, 1), col_sum))
    col_terms = lax.all_to_all(
        col_sum, "row", 0, 0, axis_index_groups=XY_GROUPS, tiled=True
    ).reshape(NX * NY, PT, WIDE)
    (row_part,) = run(
        forward_kernel, [RT], FORTH_MIB, [], (tile_count, me_too), chunks, (cids, rids, block)
    )
    row_terms = lax.all_to_all(row_part, "col", 0, 0, tiled=True).reshape(-1, PT, WIDE)
    total = col_terms.sum(axis=0) + row_terms.sum(axis=0)
    return total.reshape(PT, VEC, TILE).transpose(1, 0, 2).reshape(VEC, S).T


def solution(mesh):
    placed = (
        P(("row", "col"), None),
        P("row", "col", None, None, None),
        P("row", "col", None),
        P("row", "col", None),
        P("row", "col"),
    )
    return jax.shard_map(
        local, mesh=mesh, in_specs=placed, out_specs=P(("row", "col"), None), check_vma=False
    )
```

profile of v0, /device:TPU:57, one launch (start us, length us, event | category | flops | bytes accessed | tf_op | source)
XLA Modules:
  0.0 149.3 jit_solution(293228131979940418)
XLA Ops:
  6.5 0.0 reduce-scatter.2.cloned.1.call-start
  7.2 0.8 reshape.30
  8.0 0.1 reshape.31
  8.1 25.0 %all_gather.6.rows = f32[128,1024]{1,0:T(8,128)} all-gather(f32[8,1024]{1,0:T(8,128)S(1)} %reshape.31), channel_id=1, replica_groups={{0,1,2,3,4,5,6,7,8,9,10,11,12,13,14,15},{16,17,18,19,20,21,22,23,24,25,..., dimensions={0}, use_global_device_ids=true | all-gather | bytes 557056 | tf_op jit(solution)/shard_map/all_gather | solution.py:205
  33.1 9.9 %shard_map.55 = (f32[768,1024]{1,0:T(8,128)}, f32[16,1024]{1,0:T(8,128)}) custom-call(s32[1,1]{1,0:T(1,128)S(6)} %copy.12.count, s32[1,1]{1,0:T(1,128)} %bitcast.row, s32[1,1]{1,0:T(1,128)} %bitcast.1.col, f32[128,1024]{1,0:T(8,128)} %all_gather.6.rows, s32[1,256]{1,0:T(1,128)} %bitcast.15, s32[1,256]{1,0:T(1,128)} %bitcast.17, f32[64,64,256]{2,1,0:T(8,128)} %bitcast.23), custom_call_target="tpu_custom_call" | custom-call | flops 10000000000 | bytes 8388608 | tf_op jit(solution)/shard_map/pallas_call | solution.py:176
  43.0 0.0 copy-start
  43.0 0.0 copy-start.1
  43.0 0.0 reduce-scatter.2.cloned.1.call-update
  43.0 28.3 %all_gather.7.refs_0_ = f32[192,1024]{1,0:T(8,128)S(1)} all-gather(f32[16,1024]{1,0:T(8,128)} %get-tuple-element.12), channel_id=1, replica_groups={{0,64,128,192,256,320,384,448,512,576,640,704},{8,72,136,200,264,328,39..., dimensions={0}, use_global_device_ids=true | all-gather | bytes 851968 | tf_op jit(solution)/shard_map/all_gather | solution.py:221
  71.4 0.9 fusion
  72.3 4.4 %collective-permute-start.3 = (f32[96,1024]{1,0:T(8,128)}, f32[96,1024]{1,0:T(8,128)S(1)}, u32[]{:S(2)}, u32[]{:S(2)}) collective-permute-start(f32[96,1024]{1,0:T(8,128)} %get-tuple-element.13), channel_id=1, source_target_pairs={{0,48},{8,56},{16,0},{24,8},{32,16},{40,24},{48,32},{56,40},{64,11... | collective-permute-start | bytes 1179656 | tf_op jit(solution)/shard_map/ppermute | solution.py:230
  76.7 1.9 %collective-permute-start = (f32[96,1024]{1,0:T(8,128)}, f32[96,1024]{1,0:T(8,128)S(1)}, u32[]{:S(2)}, u32[]{:S(2)}) collective-permute-start(f32[96,1024]{1,0:T(8,128)} %get-tuple-element.14), channel_id=1, source_target_pairs={{0,16},{8,24},{16,32},{24,40},{32,48},{40,56},{48,0},{56,8},{64,80... | collective-permute-start | bytes 1179656 | tf_op jit(solution)/shard_map/ppermute | solution.py:229
  78.7 2.1 %collective-permute-start.1 = (f32[96,1024]{1,0:T(8,128)}, f32[96,1024]{1,0:T(8,128)S(1)}, u32[]{:S(2)}, u32[]{:S(2)}) collective-permute-start(f32[96,1024]{1,0:T(8,128)} %get-tuple-element.13), channel_id=1, source_target_pairs={{0,16},{8,24},{16,32},{24,40},{32,48},{40,56},{48,0},{56,8},{64,80... | collective-permute-start | bytes 1179656 | tf_op jit(solution)/shard_map/ppermute | solution.py:231
  80.7 4.4 %collective-permute-start.5 = (f32[96,1024]{1,0:T(8,128)}, f32[96,1024]{1,0:T(8,128)S(1)}, u32[]{:S(2)}, u32[]{:S(2)}) collective-permute-start(f32[96,1024]{1,0:T(8,128)} %get-tuple-element.14), channel_id=1, source_target_pairs={{0,48},{8,56},{16,0},{24,8},{32,16},{40,24},{48,32},{56,40},{64,11... | collective-permute-start | bytes 1179656 | tf_op jit(solution)/shard_map/ppermute | solution.py:232
  85.2 0.0 collective-permute-done.3.refs_6_
  85.2 3.4 %collective-permute-start.4 = (f32[96,1024]{1,0:T(8,128)S(1)}, f32[96,1024]{1,0:T(8,128)S(1)}, u32[]{:S(2)}, u32[]{:S(2)}) collective-permute-start(f32[96,1024]{1,0:T(8,128)S(1)} %collective-permute-done.3.refs_6_), channel_id=1, source_target_pairs={{0,48},{8,56},{16,0},{24,8},{32,16},{40,24},{48,32},{56,40},{64,11... | collective-permute-start | bytes 1179656 | tf_op jit(solution)/shard_map/ppermute | solution.py:234
  88.6 0.0 collective-permute-done.refs_1_
  88.6 1.9 %collective-permute-start.2 = (f32[96,1024]{1,0:T(8,128)S(1)}, f32[96,1024]{1,0:T(8,128)S(1)}, u32[]{:S(2)}, u32[]{:S(2)}) collective-permute-start(f32[96,1024]{1,0:T(8,128)S(1)} %collective-permute-done.refs_1_), channel_id=1, source_target_pairs={{0,16},{8,24},{16,32},{24,40},{32,48},{40,56},{48,0},{56,8},{64,80... | collective-permute-start | bytes 1179656 | tf_op jit(solution)/shard_map/ppermute | solution.py:233
  90.5 11.6 %reduce-scatter.2.cloned.1.call-done = f32[64,1024]{1,0:T(8,128)} async-done(((f32[768,1024]{1,0:T(8,128)}), f32[64,1024]{1,0:T(8,128)}) %reduce-scatter.2.cloned.1.call-update) | async-done | bytes 262160 | tf_op jit(solution)/shard_map/reduce_scatter | solution.py:217
  102.1 8.5 %all-to-all-start = ((f32[8,8,1024]{2,1,0:T(8,128)}), f32[8,8,1024]{2,1,0:T(8,128)S(1)}, u32[]{:S(2)}, u32[]{:S(2)}) async-start(f32[8,8,1024]{2,1,0:T(8,128)} %bitcast.19), calls=%async_computation.1 | async-start | bytes 524288 | tf_op jit(solution)/shard_map/all_to_all | solution.py:237
  110.7 0.0 collective-permute-done.1.refs_2_
  110.7 0.0 collective-permute-done.5.refs_5_
  110.7 0.0 collective-permute-done.4.refs_4_
  110.7 0.0 collective-permute-done.2.refs_3_
  110.7 0.0 copy-done
  110.7 0.0 copy-done.1
  110.7 9.4 %shard_map.56 = f32[64,1024]{1,0:T(8,128)} custom-call(s32[1,1]{1,0:T(1,128)S(6)} %copy.12.count, s32[1,1]{1,0:T(1,128)} %bitcast.row, f32[192,1024]{1,0:T(8,128)S(1)} %all_gather.7.refs_0_, f32[96,1024]{1,0:T(8,128)S(1)} %collective-permute-done.refs_1_, f32[96,1024]{1,0:T(8,128)S(1)} %collective-permute-done.1.refs_2_, ...), custom_call_target="tpu_custom_call" | custom-call | flops 10000000000 | bytes 8388608 | tf_op jit(solution)/shard_map/pallas_call | solution.py:176
  120.1 0.0 all-to-all-done
  120.2 14.4 %all-to-all-start.1 = ((f32[8,8,1024]{2,1,0:T(8,128)}), f32[8,8,1024]{2,1,0:T(8,128)S(1)}, u32[]{:S(2)}, u32[]{:S(2)}) async-start(f32[8,8,1024]{2,1,0:T(8,128)} %bitcast.10), calls=%async_computation.2 | async-start | bytes 524288 | tf_op jit(solution)/shard_map/all_to_all | solution.py:243
  134.6 7.0 %all-to-all-done.1 = f32[8,8,1024]{2,1,0:T(8,128)S(1)} async-done(((f32[8,8,1024]{2,1,0:T(8,128)}), f32[8,8,1024]{2,1,0:T(8,128)S(1)}, u32[]{:S(2)}, u32[]{:S(2)}) %all-to-all-start.1) | async-done | bytes 262176 | tf_op jit(solution)/shard_map/all_to_all | solution.py:243
  141.6 0.1 add.10
  141.8 0.7 reshape.32
  (5 shorter events, 0.1 us)
Async XLA Ops:
  6.5 95.6 %reduce-scatter.2.cloned.1.call-start = ((), (), s32[]{:S(2)}) async-start(), calls=%async_computation.3 | async-start | bytes 3407872 | tf_op jit(solution)/shard_map/reduce_scatter | solution.py:217
  43.0 67.7 %copy-start = (s32[1,1,256]{2,1,0:T(1,128)S(1)}, s32[1,1,256]{2,1,0:T(1,128)}, u32[]{:S(2)}) copy-start(s32[1,1,256]{2,1,0:T(1,128)} %param.7) | copy-start | bytes 3076
  43.0 67.7 %copy-start.1 = (s32[1,1,256]{2,1,0:T(1,128)S(1)}, s32[1,1,256]{2,1,0:T(1,128)}, u32[]{:S(2)}) copy-start(s32[1,1,256]{2,1,0:T(1,128)} %param.8) | copy-start | bytes 3076
  72.3 12.9 %collective-permute-start.3 = (f32[96,1024]{1,0:T(8,128)}, f32[96,1024]{1,0:T(8,128)S(1)}, u32[]{:S(2)}, u32[]{:S(2)}) collective-permute-start(f32[96,1024]{1,0:T(8,128)} %get-tuple-element.13), channel_id=1, source_target_pairs={{0,48},{8,56},{16,0},{24,8},{32,16},{40,24},{48,32},{56,40},{64,11... | collective-permute-start | bytes 1179656 | tf_op jit(solution)/shard_map/ppermute | solution.py:230
  76.7 11.8 %collective-permute-start = (f32[96,1024]{1,0:T(8,128)}, f32[96,1024]{1,0:T(8,128)S(1)}, u32[]{:S(2)}, u32[]{:S(2)}) collective-permute-start(f32[96,1024]{1,0:T(8,128)} %get-tuple-element.14), channel_id=1, source_target_pairs={{0,16},{8,24},{16,32},{24,40},{32,48},{40,56},{48,0},{56,8},{64,80... | collective-permute-start | bytes 1179656 | tf_op jit(solution)/shard_map/ppermute | solution.py:229
  78.7 32.0 %collective-permute-start.1 = (f32[96,1024]{1,0:T(8,128)}, f32[96,1024]{1,0:T(8,128)S(1)}, u32[]{:S(2)}, u32[]{:S(2)}) collective-permute-start(f32[96,1024]{1,0:T(8,128)} %get-tuple-element.13), channel_id=1, source_target_pairs={{0,16},{8,24},{16,32},{24,40},{32,48},{40,56},{48,0},{56,8},{64,80... | collective-permute-start | bytes 1179656 | tf_op jit(solution)/shard_map/ppermute | solution.py:231
  80.7 30.0 %collective-permute-start.5 = (f32[96,1024]{1,0:T(8,128)}, f32[96,1024]{1,0:T(8,128)S(1)}, u32[]{:S(2)}, u32[]{:S(2)}) collective-permute-start(f32[96,1024]{1,0:T(8,128)} %get-tuple-element.14), channel_id=1, source_target_pairs={{0,48},{8,56},{16,0},{24,8},{32,16},{40,24},{48,32},{56,40},{64,11... | collective-permute-start | bytes 1179656 | tf_op jit(solution)/shard_map/ppermute | solution.py:232
  85.2 25.5 %collective-permute-start.4 = (f32[96,1024]{1,0:T(8,128)S(1)}, f32[96,1024]{1,0:T(8,128)S(1)}, u32[]{:S(2)}, u32[]{:S(2)}) collective-permute-start(f32[96,1024]{1,0:T(8,128)S(1)} %collective-permute-done.3.refs_6_), channel_id=1, source_target_pairs={{0,48},{8,56},{16,0},{24,8},{32,16},{40,24},{48,32},{56,40},{64,11... | collective-permute-start | bytes 1179656 | tf_op jit(solution)/shard_map/ppermute | solution.py:234
  88.6 22.1 %collective-permute-start.2 = (f32[96,1024]{1,0:T(8,128)S(1)}, f32[96,1024]{1,0:T(8,128)S(1)}, u32[]{:S(2)}, u32[]{:S(2)}) collective-permute-start(f32[96,1024]{1,0:T(8,128)S(1)} %collective-permute-done.refs_1_), channel_id=1, source_target_pairs={{0,16},{8,24},{16,32},{24,40},{32,48},{40,56},{48,0},{56,8},{64,80... | collective-permute-start | bytes 1179656 | tf_op jit(solution)/shard_map/ppermute | solution.py:233
  102.1 18.0 %all-to-all-start = ((f32[8,8,1024]{2,1,0:T(8,128)}), f32[8,8,1024]{2,1,0:T(8,128)S(1)}, u32[]{:S(2)}, u32[]{:S(2)}) async-start(f32[8,8,1024]{2,1,0:T(8,128)} %bitcast.19), calls=%async_computation.1 | async-start | bytes 524288 | tf_op jit(solution)/shard_map/all_to_all | solution.py:237
  120.2 21.5 %all-to-all-start.1 = ((f32[8,8,1024]{2,1,0:T(8,128)}), f32[8,8,1024]{2,1,0:T(8,128)S(1)}, u32[]{:S(2)}, u32[]{:S(2)}) async-start(f32[8,8,1024]{2,1,0:T(8,128)} %bitcast.10), calls=%async_computation.2 | async-start | bytes 524288 | tf_op jit(solution)/shard_map/all_to_all | solution.py:243
Sparse Core Ops, SparseCore 0:
  43.2 58.9 reduce-scatter.1
where the time goes:
time: 151 us; the launch traced here: 149 us
  blocking collectives  53.3 us (35%)
  starting transfers between devices  41 us (27%)
  Pallas kernels  19.3 us (13%)
  waiting for transfers between devices  18.7 us (12%)
  between operations  14.2 us (9%)
  local copies, waits for them, and re-layouts  2.68 us (2%)
    all_gather x1, blocking collectives, local(): lax.all_gather(pair, 'row', axis_index_groups=Z_GROUPS, axis=0, tiled=True)  28.3 us
    all_gather x1, blocking collectives, local(): lax.all_gather(piece, ('row', 'col'), axis_index_groups=RING_GROUPS, axis...  25 us
    pallas_call x2, Pallas kernels, run(): pl.pallas_call(kernel, out_shape=[jax.ShapeDtypeStruct((rows, WIDE), jnp....  19.3 us
    all_to_all x1, starting transfers between devices, local(): lax.all_to_all(row_part, 'col', 0, 0, tiled=True).reshape(-1, PT, WIDE)  14.4 us
    reduce_scatter x1, waiting for transfers between devices, local(): lax.psum_scatter(col_part, 'row', axis_index_groups=Z_GROUPS, scatter_dim...  11.6 us
    all_to_all x1, starting transfers between devices, local(): lax.all_to_all(col_sum, 'row', 0, 0, axis_index_groups=XY_GROUPS, tiled=T...  8.55 us
    all_to_all x1, waiting for transfers between devices, local(): lax.all_to_all(row_part, 'col', 0, 0, tiled=True).reshape(-1, PT, WIDE)  7.04 us
    ppermute x1, starting transfers between devices, local(): right_first = lax.ppermute(first, 'row', row_shift(dx=-1))  4.44 us
  transfers between devices with their start and end apart: 9, of which 2 were waited for; matrix products, arithmetic and copies ran while one was open for 1% of the time, Pallas kernels for 6%

commit v1 on v0

--- a/solution.py
+++ b/solution.py
@@ -12,7 +12,7 @@
 RT = 64
 CT = 768
 NZ, NX, NY = 12, 4, 2
-NCOL = 8
+NCOL, NYL = 8, 4
 PT = S // TILE
 WIDE = VEC * TILE
 CHUNK = CT // NX
@@ -24,6 +24,12 @@
 
 def row_index(z, x, y):
     return ((z % NZ) * NX + (x % NX)) * NY + (y % NY)
+
+
+def col_shift(dy=0, core=0):
+    return [
+        (y * 2 + k, ((y + dy) % NYL) * 2 + (k ^ core)) for y in range(NYL) for k in range(2)
+    ]
 
 
 def row_shift(dx=0, dy=0):
@@ -137,9 +143,9 @@
         copy.wait()
 
 
-def forward_kernel(count, row, *refs):
+def forward_kernel(count, row, col, *refs):
     chunks, refs = refs[:CHUNKS], refs[CHUNKS:]
-    cids_far, rids_far, far, out, cids, rids, tiles, arrived, picked, summed = refs
+    cids_far, rids_far, far, own, mate, cids, rids, tiles, arrived, picked, summed = refs
     copies = fetch([(cids_far, cids), (rids_far, rids), (far, tiles)], arrived)
     for copy in copies[:2]:
         copy.wait()
@@ -149,7 +155,10 @@
     side = jnp.concatenate([chunk[...] for chunk in chunks])
     pick(picked, indicator(iota((CT, TPD), 0) == places), side)
     live = iota((1, TPD), 1) < count[0, 0]
-    at_row = indicator((iota((RT, TPD), 0) == rids[...]) & live)
+    tile, me = rids[...], col[0, 0]
+    core, y = ((tile >> 3) ^ me) & 1, ((tile >> 4) - (me >> 1)) & 3
+    places = core * (RT // 2) + y * PT + (tile & 7)
+    at_row = indicator((iota((RT, TPD), 0) == places) & live)
     copies[2].wait()
     for group in range(VEC // GROUP):
         for half in range(TPD // LANES):
@@ -168,7 +177,9 @@
                 return carry
 
             lax.fori_loop(0, TILE, step, 0, unroll=64)
-        out[:, group * GROUP * TILE : (group + 1) * GROUP * TILE] = place(at_row, whole(summed))
+        columns = slice(group * GROUP * TILE, (group + 1) * GROUP * TILE)
+        sums = place(at_row, whole(summed))
+        own[:, columns], mate[:, columns] = sums[: RT // 2], sums[RT // 2 :]
 
 
 def run(kernel, outs, vmem_mib, scratch, scalars, near, far):
@@ -179,7 +190,7 @@
         in_specs=[pl.BlockSpec(memory_space=pltpu.SMEM)] * len(scalars)
         + [in_vmem] * len(near)
         + [in_hbm] * len(far),
-        out_specs=[in_vmem] + [in_hbm] * (len(outs) - 1),
+        out_specs=[in_vmem] + [in_hbm if scratch else in_vmem] * (len(outs) - 1),
         scratch_shapes=scratch
         + [
             pltpu.VMEM((1, TPD), jnp.int32),
@@ -233,15 +244,25 @@
     far_first = lax.ppermute(left_first, "row", row_shift(dx=1))
     far_second = lax.ppermute(right_second, "row", row_shift(dx=-1))
     chunks = [mine, left_first, left_second, far_first, far_second, right_first, right_second]
-    me_too, col_sum = lax.optimization_barrier((me.reshape(1, 1), col_sum))
+    own, others = run(
+        forward_kernel,
+        [RT // 2, RT // 2],
+        FORTH_MIB,
+        [],
+        (tile_count, me.reshape(1, 1), me_col.reshape(1, 1)),
+        chunks,
+        (cids, rids, block),
+    )
+    own, col_sum = lax.optimization_barrier((own, col_sum))
     col_terms = lax.all_to_all(
         col_sum, "row", 0, 0, axis_index_groups=XY_GROUPS, tiled=True
     ).reshape(NX * NY, PT, WIDE)
-    (row_part,) = run(
-        forward_kernel, [RT], FORTH_MIB, [], (tile_count, me_too), chunks, (cids, rids, block)
-    )
-    row_terms = lax.all_to_all(row_part, "col", 0, 0, tiled=True).reshape(-1, PT, WIDE)
-    total = col_terms.sum(axis=0) + row_terms.sum(axis=0)
+    mate = lax.ppermute(others, "col", col_shift(core=1))
+    halves = (own + mate).reshape(NYL, PT, WIDE)
+    row_total = halves[0]
+    for d in range(1, NYL):
+        row_total = row_total + lax.ppermute(halves[d], "col", col_shift(dy=d))
+    total = col_terms.sum(axis=0) + row_total
     return total.reshape(PT, VEC, TILE).transpose(1, 0, 2).reshape(VEC, S).T
 
 

time: 151 us -> 151 us (level)
  starting transfers between devices: 41 us -> 43.7 us
  waiting for transfers between devices: 18.7 us -> 16.1 us
    ppermute x0 -> x4, starting transfers between devices: none -> 18 us  [the longest x3 10 us: local(): row_total = row_total + lax.ppermute(halves[d], 'col', col_shift(dy=d))]
    all_to_all x1 -> x0, starting transfers between devices: 14.4 us -> none  [local(): lax.all_to_all(row_part, 'col', 0, 0, tiled=True).reshape(-1, PT, WIDE)]
    reduce_scatter x1, waiting for transfers between devices: 11.6 us -> 0.02 us  [local(): lax.psum_scatter(col_part, 'row', axis_index_groups=Z_GROUPS, scatter_dim...]
    ppermute x1, waiting for transfers between devices: 0.01 us -> 7.78 us  [local(): far_second = lax.ppermute(right_second, 'row', row_shift(dx=-1))]
    all_to_all x1 -> x0, waiting for transfers between devices: 7.04 us -> none  [local(): lax.all_to_all(row_part, 'col', 0, 0, tiled=True).reshape(-1, PT, WIDE)]
    ppermute x0 -> x4, waiting for transfers between devices: none -> 3.8 us  [the longest x3 2.83 us: local(): row_total = row_total + lax.ppermute(halves[d], 'col', col_shift(dy=d))]
    ppermute x1, waiting for transfers between devices: 0.01 us -> 2.55 us  [local(): far_first = lax.ppermute(left_first, 'row', row_shift(dx=1))]
  transfers between devices with their start and end apart: 9 -> 12, of which waited for: 2 -> 7; matrix products, arithmetic and copies ran while one was open for 1% -> 0% of each run, Pallas kernels for 6% -> 6%
where the time goes in v1:
time: 151 us; the launch traced here: 148 us
  blocking collectives  53.3 us (35%)
  starting transfers between devices  43.7 us (29%)
  Pallas kernels  18.6 us (12%)
  waiting for transfers between devices  16.1 us (11%)
  between operations  14.2 us (9%)
  local copies, waits for them, and re-layouts  1.82 us (1%)
    all_gather x1, blocking collectives, local(): lax.all_gather(pair, 'row', axis_index_groups=Z_GROUPS, axis=0, tiled=True)  28.3 us
    all_gather x1, blocking collectives, local(): lax.all_gather(piece, ('row', 'col'), axis_index_groups=RING_GROUPS, axis...  25 us
    pallas_call x2, Pallas kernels, run(): pl.pallas_call(kernel, out_shape=[jax.ShapeDtypeStruct((rows, WIDE), jnp....  18.6 us
    ppermute x3, starting transfers between devices, local(): row_total = row_total + lax.ppermute(halves[d], 'col', col_shift(dy=d))  10 us
    ppermute x1, starting transfers between devices, local(): mate = lax.ppermute(others, 'col', col_shift(core=1))  7.93 us
    ppermute x1, waiting for transfers between devices, local(): far_second = lax.ppermute(right_second, 'row', row_shift(dx=-1))  7.78 us
    all_to_all x1, starting transfers between devices, local(): lax.all_to_all(col_sum, 'row', 0, 0, axis_index_groups=XY_GROUPS, tiled=T...  7.4 us
    ppermute x1, starting transfers between devices, local(): right_first = lax.ppermute(first, 'row', row_shift(dx=-1))  4.44 us
  transfers between devices with their start and end apart: 12, of which 7 were waited for; matrix products, arithmetic and copies ran while one was open for 0% of the time, Pallas kernels for 6%

profile of v1, /device:TPU:57, one launch (start us, length us, event | category | flops | bytes accessed | tf_op | source)
XLA Modules:
  0.0 147.8 jit_solution(11081917516896171333)
XLA Ops:
  6.5 0.0 reduce-scatter.2.cloned.1.call-start
  7.2 0.8 reshape.35
  8.0 0.1 reshape.36
  8.1 25.0 %all_gather.6.rows = f32[128,1024]{1,0:T(8,128)} all-gather(f32[8,1024]{1,0:T(8,128)S(1)} %reshape.36), channel_id=1, replica_groups={{0,1,2,3,4,5,6,7,8,9,10,11,12,13,14,15},{16,17,18,19,20,21,22,23,24,25,..., dimensions={0}, use_global_device_ids=true | all-gather | bytes 557056 | tf_op jit(solution)/shard_map/all_gather | solution.py:216
  33.1 9.9 %shard_map.55 = (f32[768,1024]{1,0:T(8,128)}, f32[16,1024]{1,0:T(8,128)}) custom-call(s32[1,1]{1,0:T(1,128)S(6)} %copy.10.count, s32[1,1]{1,0:T(1,128)} %bitcast.row, s32[1,1]{1,0:T(1,128)} %bitcast.1.col, f32[128,1024]{1,0:T(8,128)} %all_gather.6.rows, s32[1,256]{1,0:T(1,128)} %bitcast.14, s32[1,256]{1,0:T(1,128)} %bitcast.16, f32[64,64,256]{2,1,0:T(8,128)} %bitcast.22), custom_call_target="tpu_custom_call" | custom-call | flops 10000000000 | bytes 8388608 | tf_op jit(solution)/shard_map/pallas_call | solution.py:187
  43.0 0.0 copy-start
  43.0 0.0 copy-start.1
  43.0 0.0 reduce-scatter.2.cloned.1.call-update
  43.1 28.3 %all_gather.7.refs_0_ = f32[192,1024]{1,0:T(8,128)S(1)} all-gather(f32[16,1024]{1,0:T(8,128)} %get-tuple-element.11), channel_id=1, replica_groups={{0,64,128,192,256,320,384,448,512,576,640,704},{8,72,136,200,264,328,39..., dimensions={0}, use_global_device_ids=true | all-gather | bytes 851968 | tf_op jit(solution)/shard_map/all_gather | solution.py:232
  71.4 0.1 fusion.3
  71.5 4.4 %collective-permute-start.3 = (f32[96,1024]{1,0:T(8,128)S(1)}, f32[96,1024]{1,0:T(8,128)S(1)}, u32[]{:S(2)}, u32[]{:S(2)}) collective-permute-start(f32[96,1024]{1,0:T(8,128)S(1)} %get-tuple-element.17), channel_id=1, source_target_pairs={{0,48},{8,56},{16,0},{24,8},{32,16},{40,24},{48,32},{56,40},{64,11... | collective-permute-start | bytes 1179656 | tf_op jit(solution)/shard_map/ppermute | solution.py:241
  75.9 1.9 %collective-permute-start = (f32[96,1024]{1,0:T(8,128)S(1)}, f32[96,1024]{1,0:T(8,128)S(1)}, u32[]{:S(2)}, u32[]{:S(2)}) collective-permute-start(f32[96,1024]{1,0:T(8,128)S(1)} %get-tuple-element.18), channel_id=1, source_target_pairs={{0,16},{8,24},{16,32},{24,40},{32,48},{40,56},{48,0},{56,8},{64,80... | collective-permute-start | bytes 1179656 | tf_op jit(solution)/shard_map/ppermute | solution.py:240
  77.8 2.1 %collective-permute-start.1 = (f32[96,1024]{1,0:T(8,128)S(1)}, f32[96,1024]{1,0:T(8,128)S(1)}, u32[]{:S(2)}, u32[]{:S(2)}) collective-permute-start(f32[96,1024]{1,0:T(8,128)S(1)} %get-tuple-element.17), channel_id=1, source_target_pairs={{0,16},{8,24},{16,32},{24,40},{32,48},{40,56},{48,0},{56,8},{64,80... | collective-permute-start | bytes 1179656 | tf_op jit(solution)/shard_map/ppermute | solution.py:242
  79.9 4.4 %collective-permute-start.5 = (f32[96,1024]{1,0:T(8,128)S(1)}, f32[96,1024]{1,0:T(8,128)S(1)}, u32[]{:S(2)}, u32[]{:S(2)}) collective-permute-start(f32[96,1024]{1,0:T(8,128)S(1)} %get-tuple-element.18), channel_id=1, source_target_pairs={{0,48},{8,56},{16,0},{24,8},{32,16},{40,24},{48,32},{56,40},{64,11... | collective-permute-start | bytes 1179656 | tf_op jit(solution)/shard_map/ppermute | solution.py:243
  84.3 0.0 collective-permute-done.3.refs_6_
  84.3 3.4 %collective-permute-start.4 = (f32[96,1024]{1,0:T(8,128)S(1)}, f32[96,1024]{1,0:T(8,128)S(1)}, u32[]{:S(2)}, u32[]{:S(2)}) collective-permute-start(f32[96,1024]{1,0:T(8,128)S(1)} %collective-permute-done.3.refs_6_), channel_id=1, source_target_pairs={{0,48},{8,56},{16,0},{24,8},{32,16},{40,24},{48,32},{56,40},{64,11... | collective-permute-start | bytes 1179656 | tf_op jit(solution)/shard_map/ppermute | solution.py:245
  87.7 0.0 collective-permute-done.refs_1_
  87.7 2.1 %collective-permute-start.2 = (f32[96,1024]{1,0:T(8,128)S(1)}, f32[96,1024]{1,0:T(8,128)S(1)}, u32[]{:S(2)}, u32[]{:S(2)}) collective-permute-start(f32[96,1024]{1,0:T(8,128)S(1)} %collective-permute-done.refs_1_), channel_id=1, source_target_pairs={{0,16},{8,24},{16,32},{24,40},{32,48},{40,56},{48,0},{56,8},{64,80... | collective-permute-start | bytes 1179656 | tf_op jit(solution)/shard_map/ppermute | solution.py:244
  89.8 1.5 %collective-permute-done.1.refs_2_ = f32[96,1024]{1,0:T(8,128)S(1)} collective-permute-done((f32[96,1024]{1,0:T(8,128)S(1)}, f32[96,1024]{1,0:T(8,128)S(1)}, u32[]{:S(2)}, u32[]{:S(2)}) %collective-permute-start.1) | collective-permute-done | bytes 393248 | tf_op jit(solution)/shard_map/ppermute | solution.py:242
  91.3 0.5 collective-permute-done.5.refs_5_
  91.8 7.8 %collective-permute-done.4.refs_4_ = f32[96,1024]{1,0:T(8,128)S(1)} collective-permute-done((f32[96,1024]{1,0:T(8,128)S(1)}, f32[96,1024]{1,0:T(8,128)S(1)}, u32[]{:S(2)}, u32[]{:S(2)}) %collective-permute-start.4) | collective-permute-done | bytes 393248 | tf_op jit(solution)/shard_map/ppermute | solution.py:245
  99.6 2.6 %collective-permute-done.2.refs_3_ = f32[96,1024]{1,0:T(8,128)S(1)} collective-permute-done((f32[96,1024]{1,0:T(8,128)S(1)}, f32[96,1024]{1,0:T(8,128)S(1)}, u32[]{:S(2)}, u32[]{:S(2)}) %collective-permute-start.2) | collective-permute-done | bytes 393248 | tf_op jit(solution)/shard_map/ppermute | solution.py:244
  102.1 0.0 copy-done
  102.1 0.0 copy-done.1
  102.1 8.7 %shard_map.56 = (f32[32,1024]{1,0:T(8,128)S(1)}, f32[32,1024]{1,0:T(8,128)S(1)}) custom-call(s32[1,1]{1,0:T(1,128)S(6)} %copy.10.count, s32[1,1]{1,0:T(1,128)} %bitcast.row, s32[1,1]{1,0:T(1,128)} %bitcast.1.col, f32[192,1024]{1,0:T(8,128)S(1)} %all_gather.7.refs_0_, f32[96,1024]{1,0:T(8,128)S(1)} %collective-permute-done.refs_1_, ...), custom_call_target="tpu_custom_call" | custom-call | flops 10000000000 | bytes 8388608 | tf_op jit(solution)/shard_map/pallas_call | solution.py:187
  110.8 0.0 reduce-scatter.2.cloned.1.call-done
  110.9 7.4 %all-to-all-start = ((f32[8,8,1024]{2,1,0:T(8,128)}), f32[8,8,1024]{2,1,0:T(8,128)S(1)}, u32[]{:S(2)}, u32[]{:S(2)}) async-start(f32[8,8,1024]{2,1,0:T(8,128)} %bitcast.18), calls=%async_computation.1 | async-start | bytes 524288 | tf_op jit(solution)/shard_map/all_to_all | solution.py:257
  118.3 7.9 %collective-permute-start.6 = (f32[32,1024]{1,0:T(8,128)S(1)}, f32[32,1024]{1,0:T(8,128)S(1)}, u32[]{:S(2)}, u32[]{:S(2)}) collective-permute-start(f32[32,1024]{1,0:T(8,128)S(1)} %get-tuple-element.16), channel_id=1, source_target_pairs={{0,1},{1,0},{2,3},{3,2},{4,5},{5,4},{6,7},{7,6},{8,9},{9,8},{10,11... | collective-permute-start | bytes 393224 | tf_op jit(solution)/shard_map/ppermute | solution.py:260
  126.2 1.0 collective-permute-done.6
  127.2 5.1 %collective-permute-start.7 = (f32[8,1024]{1,0:T(8,128)S(1)}, f32[8,1024]{1,0:T(8,128)S(1)}, u32[]{:S(2)}, u32[]{:S(2)}) collective-permute-start(f32[8,1024]{1,0:T(8,128)S(1)} %get-tuple-element.19), channel_id=1, source_target_pairs={{0,2},{1,3},{2,4},{3,5},{4,6},{5,7},{6,0},{7,1},{8,10},{9,11},{10,... | collective-permute-start | bytes 98312 | tf_op jit(solution)/shard_map/ppermute | solution.py:264
  132.3 1.9 %collective-permute-start.9 = (f32[8,1024]{1,0:T(8,128)S(1)}, f32[8,1024]{1,0:T(8,128)S(1)}, u32[]{:S(2)}, u32[]{:S(2)}) collective-permute-start(f32[8,1024]{1,0:T(8,128)S(1)} %get-tuple-element.20), channel_id=1, source_target_pairs={{0,6},{1,7},{2,0},{3,1},{4,2},{5,3},{6,4},{7,5},{8,14},{9,15},{10,... | collective-permute-start | bytes 98312 | tf_op jit(solution)/shard_map/ppermute | solution.py:264
  134.2 3.0 %collective-permute-start.8 = (f32[8,1024]{1,0:T(8,128)S(1)}, f32[8,1024]{1,0:T(8,128)S(1)}, u32[]{:S(2)}, u32[]{:S(2)}) collective-permute-start(f32[8,1024]{1,0:T(8,128)S(1)} %get-tuple-element.21), channel_id=1, source_target_pairs={{0,4},{1,5},{2,6},{3,7},{4,0},{5,1},{6,2},{7,3},{8,12},{9,13},{10,... | collective-permute-start | bytes 98312 | tf_op jit(solution)/shard_map/ppermute | solution.py:264
  137.3 0.0 all-to-all-done
  137.3 0.0 collective-permute-done.7
  137.3 1.4 collective-permute-done.9
  138.8 1.4 collective-permute-done.8
  140.2 0.1 reshape.37
  140.3 0.7 reshape.38
  (6 shorter events, 0.1 us)
Async XLA Ops:
  6.5 104.3 %reduce-scatter.2.cloned.1.call-start = ((), (), s32[]{:S(2)}) async-start(), calls=%async_computation.2 | async-start | bytes 3407872 | tf_op jit(solution)/shard_map/reduce_scatter | solution.py:228
  43.0 59.1 %copy-start = (s32[1,1,256]{2,1,0:T(1,128)S(1)}, s32[1,1,256]{2,1,0:T(1,128)}, u32[]{:S(2)}) copy-start(s32[1,1,256]{2,1,0:T(1,128)} %param.7) | copy-start | bytes 3076
  43.0 59.1 %copy-start.1 = (s32[1,1,256]{2,1,0:T(1,128)S(1)}, s32[1,1,256]{2,1,0:T(1,128)}, u32[]{:S(2)}) copy-start(s32[1,1,256]{2,1,0:T(1,128)} %param.8) | copy-start | bytes 3076
  71.5 12.9 %collective-permute-start.3 = (f32[96,1024]{1,0:T(8,128)S(1)}, f32[96,1024]{1,0:T(8,128)S(1)}, u32[]{:S(2)}, u32[]{:S(2)}) collective-permute-start(f32[96,1024]{1,0:T(8,128)S(1)} %get-tuple-element.17), channel_id=1, source_target_pairs={{0,48},{8,56},{16,0},{24,8},{32,16},{40,24},{48,32},{56,40},{64,11... | collective-permute-start | bytes 1179656 | tf_op jit(solution)/shard_map/ppermute | solution.py:241
  75.9 11.8 %collective-permute-start = (f32[96,1024]{1,0:T(8,128)S(1)}, f32[96,1024]{1,0:T(8,128)S(1)}, u32[]{:S(2)}, u32[]{:S(2)}) collective-permute-start(f32[96,1024]{1,0:T(8,128)S(1)} %get-tuple-element.18), channel_id=1, source_target_pairs={{0,16},{8,24},{16,32},{24,40},{32,48},{40,56},{48,0},{56,8},{64,80... | collective-permute-start | bytes 1179656 | tf_op jit(solution)/shard_map/ppermute | solution.py:240
  77.8 13.5 %collective-permute-start.1 = (f32[96,1024]{1,0:T(8,128)S(1)}, f32[96,1024]{1,0:T(8,128)S(1)}, u32[]{:S(2)}, u32[]{:S(2)}) collective-permute-start(f32[96,1024]{1,0:T(8,128)S(1)} %get-tuple-element.17), channel_id=1, source_target_pairs={{0,16},{8,24},{16,32},{24,40},{32,48},{40,56},{48,0},{56,8},{64,80... | collective-permute-start | bytes 1179656 | tf_op jit(solution)/shard_map/ppermute | solution.py:242
  79.9 11.9 %collective-permute-start.5 = (f32[96,1024]{1,0:T(8,128)S(1)}, f32[96,1024]{1,0:T(8,128)S(1)}, u32[]{:S(2)}, u32[]{:S(2)}) collective-permute-start(f32[96,1024]{1,0:T(8,128)S(1)} %get-tuple-element.18), channel_id=1, source_target_pairs={{0,48},{8,56},{16,0},{24,8},{32,16},{40,24},{48,32},{56,40},{64,11... | collective-permute-start | bytes 1179656 | tf_op jit(solution)/shard_map/ppermute | solution.py:243
  84.3 15.2 %collective-permute-start.4 = (f32[96,1024]{1,0:T(8,128)S(1)}, f32[96,1024]{1,0:T(8,128)S(1)}, u32[]{:S(2)}, u32[]{:S(2)}) collective-permute-start(f32[96,1024]{1,0:T(8,128)S(1)} %collective-permute-done.3.refs_6_), channel_id=1, source_target_pairs={{0,48},{8,56},{16,0},{24,8},{32,16},{40,24},{48,32},{56,40},{64,11... | collective-permute-start | bytes 1179656 | tf_op jit(solution)/shard_map/ppermute | solution.py:245
  87.7 14.4 %collective-permute-start.2 = (f32[96,1024]{1,0:T(8,128)S(1)}, f32[96,1024]{1,0:T(8,128)S(1)}, u32[]{:S(2)}, u32[]{:S(2)}) collective-permute-start(f32[96,1024]{1,0:T(8,128)S(1)} %collective-permute-done.refs_1_), channel_id=1, source_target_pairs={{0,16},{8,24},{16,32},{24,40},{32,48},{40,56},{48,0},{56,8},{64,80... | collective-permute-start | bytes 1179656 | tf_op jit(solution)/shard_map/ppermute | solution.py:244
  110.9 26.4 %all-to-all-start = ((f32[8,8,1024]{2,1,0:T(8,128)}), f32[8,8,1024]{2,1,0:T(8,128)S(1)}, u32[]{:S(2)}, u32[]{:S(2)}) async-start(f32[8,8,1024]{2,1,0:T(8,128)} %bitcast.18), calls=%async_computation.1 | async-start | bytes 524288 | tf_op jit(solution)/shard_map/all_to_all | solution.py:257
  118.3 8.9 %collective-permute-start.6 = (f32[32,1024]{1,0:T(8,128)S(1)}, f32[32,1024]{1,0:T(8,128)S(1)}, u32[]{:S(2)}, u32[]{:S(2)}) collective-permute-start(f32[32,1024]{1,0:T(8,128)S(1)} %get-tuple-element.16), channel_id=1, source_target_pairs={{0,1},{1,0},{2,3},{3,2},{4,5},{5,4},{6,7},{7,6},{8,9},{9,8},{10,11... | collective-permute-start | bytes 393224 | tf_op jit(solution)/shard_map/ppermute | solution.py:260
  127.2 10.1 %collective-permute-start.7 = (f32[8,1024]{1,0:T(8,128)S(1)}, f32[8,1024]{1,0:T(8,128)S(1)}, u32[]{:S(2)}, u32[]{:S(2)}) collective-permute-start(f32[8,1024]{1,0:T(8,128)S(1)} %get-tuple-element.19), channel_id=1, source_target_pairs={{0,2},{1,3},{2,4},{3,5},{4,6},{5,7},{6,0},{7,1},{8,10},{9,11},{10,... | collective-permute-start | bytes 98312 | tf_op jit(solution)/shard_map/ppermute | solution.py:264
  132.3 6.5 %collective-permute-start.9 = (f32[8,1024]{1,0:T(8,128)S(1)}, f32[8,1024]{1,0:T(8,128)S(1)}, u32[]{:S(2)}, u32[]{:S(2)}) collective-permute-start(f32[8,1024]{1,0:T(8,128)S(1)} %get-tuple-element.20), channel_id=1, source_target_pairs={{0,6},{1,7},{2,0},{3,1},{4,2},{5,3},{6,4},{7,5},{8,14},{9,15},{10,... | collective-permute-start | bytes 98312 | tf_op jit(solution)/shard_map/ppermute | solution.py:264
  134.2 5.9 %collective-permute-start.8 = (f32[8,1024]{1,0:T(8,128)S(1)}, f32[8,1024]{1,0:T(8,128)S(1)}, u32[]{:S(2)}, u32[]{:S(2)}) collective-permute-start(f32[8,1024]{1,0:T(8,128)S(1)} %get-tuple-element.21), channel_id=1, source_target_pairs={{0,4},{1,5},{2,6},{3,7},{4,0},{5,1},{6,2},{7,3},{8,12},{9,13},{10,... | collective-permute-start | bytes 98312 | tf_op jit(solution)/shard_map/ppermute | solution.py:264
Sparse Core Ops, SparseCore 0:
  43.2 58.9 reduce-scatter.1

commit v2 on v1

--- a/solution.py
+++ b/solution.py
@@ -18,7 +18,6 @@
 CHUNK = CT // NX
 GROUP = 4
 LANES = 128
-CHUNKS = 7
 BACK_MIB, FORTH_MIB = 58, 48
 
 
@@ -86,17 +85,14 @@
     return copies
 
 
-def pick(picked, onehot, value):
-    dims = (((0,), (0,)), ((), ()))
-    put(
-        picked,
-        lax.dot_general(
-            jnp.concatenate(three_parts(value)),
-            jnp.concatenate([onehot] * 3),
-            dims,
-            preferred_element_type=jnp.float32,
-        ),
-    )
+def pick(picked, onehot, value, before=None):
+    found = lax.dot_general(
+        jnp.concatenate(three_parts(value)),
+        jnp.concatenate([onehot] * 3),
+        (((0,), (0,)), ((), ())),
+        preferred_element_type=jnp.float32,
+    )
+    put(picked, found if before is None else found + whole(before))
 
 
 def place(onehot, value):
@@ -143,17 +139,28 @@
         copy.wait()
 
 
+def places_of(tile, row):
+    x, rest = (tile >> 4) & 3, (tile >> 6) * (NY * PT) + (tile & 15)
+    return (((row >> 1) - x) & 3) * CHUNK + rest
+
+
+def near_kernel(row, *refs):
+    chunks, (cids, found) = refs[:-2], refs[-2:]
+    places = places_of(cids[...], row[0, 0])
+    places = jnp.where(places < 2 * CHUNK, places, jnp.where(places < 3 * CHUNK, -1, places - CHUNK))
+    side = jnp.concatenate([chunk[...] for chunk in chunks])
+    pick(found, indicator(iota((3 * CHUNK, TPD), 0) == places), side)
+
+
 def forward_kernel(count, row, col, *refs):
-    chunks, refs = refs[:CHUNKS], refs[CHUNKS:]
+    found, far_first, far_second, refs = *refs[:3], refs[3:]
     cids_far, rids_far, far, own, mate, cids, rids, tiles, arrived, picked, summed = refs
     copies = fetch([(cids_far, cids), (rids_far, rids), (far, tiles)], arrived)
     for copy in copies[:2]:
         copy.wait()
-    tile = cids[...]
-    x, rest = (tile >> 4) & 3, (tile >> 6) * (NY * PT) + (tile & 15)
-    places = (((row[0, 0] >> 1) - x) & 3) * CHUNK + rest
-    side = jnp.concatenate([chunk[...] for chunk in chunks])
-    pick(picked, indicator(iota((CT, TPD), 0) == places), side)
+    places = places_of(cids[...], row[0, 0]) - 2 * CHUNK
+    side = jnp.concatenate([far_first[...], far_second[...]])
+    pick(picked, indicator(iota((CHUNK, TPD), 0) == places), side, found)
     live = iota((1, TPD), 1) < count[0, 0]
     tile, me = rids[...], col[0, 0]
     core, y = ((tile >> 3) ^ me) & 1, ((tile >> 4) - (me >> 1)) & 3
@@ -243,14 +250,21 @@
     right_first = lax.ppermute(first, "row", row_shift(dx=-1))
     far_first = lax.ppermute(left_first, "row", row_shift(dx=1))
     far_second = lax.ppermute(right_second, "row", row_shift(dx=-1))
-    chunks = [mine, left_first, left_second, far_first, far_second, right_first, right_second]
+    in_vmem = pl.BlockSpec(memory_space=pltpu.VMEM)
+    found = pl.pallas_call(
+        near_kernel,
+        out_shape=jax.ShapeDtypeStruct((TPD // LANES, WIDE, LANES), jnp.float32),
+        in_specs=[pl.BlockSpec(memory_space=pltpu.SMEM)] + [in_vmem] * 6,
+        out_specs=in_vmem,
+        compiler_params=pltpu.CompilerParams(vmem_limit_bytes=FORTH_MIB * 1024 * 1024),
+    )(me.reshape(1, 1), mine, left_first, left_second, right_first, right_second, cids)
     own, others = run(
         forward_kernel,
         [RT // 2, RT // 2],
         FORTH_MIB,
         [],
         (tile_count, me.reshape(1, 1), me_col.reshape(1, 1)),
-        chunks,
+        (found, far_first, far_second),
         (cids, rids, block),
     )
     own, col_sum = lax.optimization_barrier((own, col_sum))

time: 151 us -> 151 us (level)
  transfers between devices with their start and end apart: 12 -> 12, of which waited for: 7 -> 7; matrix products, arithmetic and copies ran while one was open for 0% -> 0% of each run, Pallas kernels for 6% -> 7%
where the time goes in v2:
time: 151 us; the launch traced here: 148 us
  blocking collectives  53.3 us (35%)
  starting transfers between devices  43.7 us (29%)
  Pallas kernels  19.8 us (13%)
  waiting for transfers between devices  14.9 us (10%)
  between operations  14.2 us (9%)
  local copies, waits for them, and re-layouts  1.82 us (1%)
    all_gather x1, blocking collectives, local(): lax.all_gather(pair, 'row', axis_index_groups=Z_GROUPS, axis=0, tiled=True)  28.3 us
    all_gather x1, blocking collectives, local(): lax.all_gather(piece, ('row', 'col'), axis_index_groups=RING_GROUPS, axis...  25 us
    pallas_call x2, Pallas kernels, run(): pl.pallas_call(kernel, out_shape=[jax.ShapeDtypeStruct((rows, WIDE), jnp....  18.6 us
    ppermute x3, starting transfers between devices, local(): row_total = row_total + lax.ppermute(halves[d], 'col', col_shift(dy=d))  10 us
    ppermute x1, starting transfers between devices, local(): mate = lax.ppermute(others, 'col', col_shift(core=1))  7.95 us
    all_to_all x1, starting transfers between devices, local(): lax.all_to_all(col_sum, 'row', 0, 0, axis_index_groups=XY_GROUPS, tiled=T...  7.38 us
    ppermute x1, waiting for transfers between devices, local(): far_second = lax.ppermute(right_second, 'row', row_shift(dx=-1))  6.57 us
    ppermute x1, starting transfers between devices, local(): right_first = lax.ppermute(first, 'row', row_shift(dx=-1))  4.44 us
  transfers between devices with their start and end apart: 12, of which 7 were waited for; matrix products, arithmetic and copies ran while one was open for 0% of the time, Pallas kernels for 7%

profile of v2, /device:TPU:57, one launch (start us, length us, event | category | flops | bytes accessed | tf_op | source)
XLA Modules:
  0.0 147.8 jit_solution(2496393416046195541)
XLA Ops:
  6.5 0.0 reduce-scatter.2.cloned.1.call-start
  7.2 0.8 reshape.36
  8.0 0.1 reshape.37
  8.1 25.0 %all_gather.6.rows = f32[128,1024]{1,0:T(8,128)} all-gather(f32[8,1024]{1,0:T(8,128)S(1)} %reshape.37), channel_id=1, replica_groups={{0,1,2,3,4,5,6,7,8,9,10,11,12,13,14,15},{16,17,18,19,20,21,22,23,24,25,..., dimensions={0}, use_global_device_ids=true | all-gather | bytes 557056 | tf_op jit(solution)/shard_map/all_gather | solution.py:223
  33.1 9.9 %shard_map.55 = (f32[768,1024]{1,0:T(8,128)}, f32[16,1024]{1,0:T(8,128)}) custom-call(s32[1,1]{1,0:T(1,128)S(6)} %copy.10.count, s32[1,1]{1,0:T(1,128)} %bitcast.row, s32[1,1]{1,0:T(1,128)} %bitcast.1.col, f32[128,1024]{1,0:T(8,128)} %all_gather.6.rows, s32[1,256]{1,0:T(1,128)} %bitcast.17, s32[1,256]{1,0:T(1,128)} %bitcast.14, f32[64,64,256]{2,1,0:T(8,128)} %bitcast.23), custom_call_target="tpu_custom_call" | custom-call | flops 10000000000 | bytes 8388608 | tf_op jit(solution)/shard_map/pallas_call | solution.py:194
  43.0 0.0 copy-start
  43.0 0.0 copy-start.1
  43.0 0.0 reduce-scatter.2.cloned.1.call-update
  43.1 28.3 %all_gather.7.refs_0_ = f32[192,1024]{1,0:T(8,128)S(1)} all-gather(f32[16,1024]{1,0:T(8,128)} %get-tuple-element.11), channel_id=1, replica_groups={{0,64,128,192,256,320,384,448,512,576,640,704},{8,72,136,200,264,328,39..., dimensions={0}, use_global_device_ids=true | all-gather | bytes 851968 | tf_op jit(solution)/shard_map/all_gather | solution.py:239
  71.4 0.1 fusion.3
  71.5 4.4 %collective-permute-start.3 = (f32[96,1024]{1,0:T(8,128)S(1)}, f32[96,1024]{1,0:T(8,128)S(1)}, u32[]{:S(2)}, u32[]{:S(2)}) collective-permute-start(f32[96,1024]{1,0:T(8,128)S(1)} %get-tuple-element.17), channel_id=1, source_target_pairs={{0,48},{8,56},{16,0},{24,8},{32,16},{40,24},{48,32},{56,40},{64,11... | collective-permute-start | bytes 1179656 | tf_op jit(solution)/shard_map/ppermute | solution.py:248
  75.9 1.9 %collective-permute-start = (f32[96,1024]{1,0:T(8,128)S(1)}, f32[96,1024]{1,0:T(8,128)S(1)}, u32[]{:S(2)}, u32[]{:S(2)}) collective-permute-start(f32[96,1024]{1,0:T(8,128)S(1)} %get-tuple-element.18), channel_id=1, source_target_pairs={{0,16},{8,24},{16,32},{24,40},{32,48},{40,56},{48,0},{56,8},{64,80... | collective-permute-start | bytes 1179656 | tf_op jit(solution)/shard_map/ppermute | solution.py:247
  77.8 2.1 %collective-permute-start.1 = (f32[96,1024]{1,0:T(8,128)S(1)}, f32[96,1024]{1,0:T(8,128)S(1)}, u32[]{:S(2)}, u32[]{:S(2)}) collective-permute-start(f32[96,1024]{1,0:T(8,128)S(1)} %get-tuple-element.17), channel_id=1, source_target_pairs={{0,16},{8,24},{16,32},{24,40},{32,48},{40,56},{48,0},{56,8},{64,80... | collective-permute-start | bytes 1179656 | tf_op jit(solution)/shard_map/ppermute | solution.py:249
  79.9 4.4 %collective-permute-start.2 = (f32[96,1024]{1,0:T(8,128)S(1)}, f32[96,1024]{1,0:T(8,128)S(1)}, u32[]{:S(2)}, u32[]{:S(2)}) collective-permute-start(f32[96,1024]{1,0:T(8,128)S(1)} %get-tuple-element.18), channel_id=1, source_target_pairs={{0,48},{8,56},{16,0},{24,8},{32,16},{40,24},{48,32},{56,40},{64,11... | collective-permute-start | bytes 1179656 | tf_op jit(solution)/shard_map/ppermute | solution.py:250
  84.3 0.0 collective-permute-done.3.refs_4_
  84.3 3.4 %collective-permute-start.5 = (f32[96,1024]{1,0:T(8,128)S(1)}, f32[96,1024]{1,0:T(8,128)S(1)}, u32[]{:S(2)}, u32[]{:S(2)}) collective-permute-start(f32[96,1024]{1,0:T(8,128)S(1)} %collective-permute-done.3.refs_4_), channel_id=1, source_target_pairs={{0,48},{8,56},{16,0},{24,8},{32,16},{40,24},{48,32},{56,40},{64,11... | collective-permute-start | bytes 1179656 | tf_op jit(solution)/shard_map/ppermute | solution.py:252
  87.7 0.0 collective-permute-done.refs_1_
  87.7 2.1 %collective-permute-start.4 = (f32[96,1024]{1,0:T(8,128)S(1)}, f32[96,1024]{1,0:T(8,128)S(1)}, u32[]{:S(2)}, u32[]{:S(2)}) collective-permute-start(f32[96,1024]{1,0:T(8,128)S(1)} %collective-permute-done.refs_1_), channel_id=1, source_target_pairs={{0,16},{8,24},{16,32},{24,40},{32,48},{40,56},{48,0},{56,8},{64,80... | collective-permute-start | bytes 1179656 | tf_op jit(solution)/shard_map/ppermute | solution.py:251
  89.8 1.5 %collective-permute-done.1.refs_2_ = f32[96,1024]{1,0:T(8,128)S(1)} collective-permute-done((f32[96,1024]{1,0:T(8,128)S(1)}, f32[96,1024]{1,0:T(8,128)S(1)}, u32[]{:S(2)}, u32[]{:S(2)}) %collective-permute-start.1) | collective-permute-done | bytes 393248 | tf_op jit(solution)/shard_map/ppermute | solution.py:249
  91.3 0.5 collective-permute-done.2.refs_3_
  91.8 0.0 copy-done
  91.8 1.2 shard_map.56.refs_0_
  93.0 6.6 %collective-permute-done.5.refs_2_ = f32[96,1024]{1,0:T(8,128)S(1)} collective-permute-done((f32[96,1024]{1,0:T(8,128)S(1)}, f32[96,1024]{1,0:T(8,128)S(1)}, u32[]{:S(2)}, u32[]{:S(2)}) %collective-permute-start.5) | collective-permute-done | bytes 393248 | tf_op jit(solution)/shard_map/ppermute | solution.py:252
  99.6 2.6 %collective-permute-done.4.refs_1_ = f32[96,1024]{1,0:T(8,128)S(1)} collective-permute-done((f32[96,1024]{1,0:T(8,128)S(1)}, f32[96,1024]{1,0:T(8,128)S(1)}, u32[]{:S(2)}, u32[]{:S(2)}) %collective-permute-start.4) | collective-permute-done | bytes 393248 | tf_op jit(solution)/shard_map/ppermute | solution.py:251
  102.1 0.0 copy-done.1
  102.1 8.7 %shard_map.57 = (f32[32,1024]{1,0:T(8,128)S(1)}, f32[32,1024]{1,0:T(8,128)S(1)}) custom-call(s32[1,1]{1,0:T(1,128)S(6)} %copy.10.count, s32[1,1]{1,0:T(1,128)} %bitcast.row, s32[1,1]{1,0:T(1,128)} %bitcast.1.col, f32[2,1024,128]{2,1,0:T(8,128)S(1)} %shard_map.56.refs_0_, f32[96,1024]{1,0:T(8,128)S(1)} %collective-permute-done.4.refs_1_, ...), custom_call_target="tpu_custom_call" | custom-call | flops 10000000000 | bytes 8388608 | tf_op jit(solution)/shard_map/pallas_call | solution.py:194
  110.8 0.0 reduce-scatter.2.cloned.1.call-done
  110.9 7.4 %all-to-all-start = ((f32[8,8,1024]{2,1,0:T(8,128)}), f32[8,8,1024]{2,1,0:T(8,128)S(1)}, u32[]{:S(2)}, u32[]{:S(2)}) async-start(f32[8,8,1024]{2,1,0:T(8,128)} %bitcast.19), calls=%async_computation.1 | async-start | bytes 524288 | tf_op jit(solution)/shard_map/all_to_all | solution.py:271
  118.2 7.9 %collective-permute-start.6 = (f32[32,1024]{1,0:T(8,128)S(1)}, f32[32,1024]{1,0:T(8,128)S(1)}, u32[]{:S(2)}, u32[]{:S(2)}) collective-permute-start(f32[32,1024]{1,0:T(8,128)S(1)} %get-tuple-element.16), channel_id=1, source_target_pairs={{0,1},{1,0},{2,3},{3,2},{4,5},{5,4},{6,7},{7,6},{8,9},{9,8},{10,11... | collective-permute-start | bytes 393224 | tf_op jit(solution)/shard_map/ppermute | solution.py:274
  126.2 1.0 collective-permute-done.6
  127.2 5.1 %collective-permute-start.7 = (f32[8,1024]{1,0:T(8,128)S(1)}, f32[8,1024]{1,0:T(8,128)S(1)}, u32[]{:S(2)}, u32[]{:S(2)}) collective-permute-start(f32[8,1024]{1,0:T(8,128)S(1)} %get-tuple-element.19), channel_id=1, source_target_pairs={{0,2},{1,3},{2,4},{3,5},{4,6},{5,7},{6,0},{7,1},{8,10},{9,11},{10,... | collective-permute-start | bytes 98312 | tf_op jit(solution)/shard_map/ppermute | solution.py:278
  132.3 1.9 %collective-permute-start.9 = (f32[8,1024]{1,0:T(8,128)S(1)}, f32[8,1024]{1,0:T(8,128)S(1)}, u32[]{:S(2)}, u32[]{:S(2)}) collective-permute-start(f32[8,1024]{1,0:T(8,128)S(1)} %get-tuple-element.20), channel_id=1, source_target_pairs={{0,6},{1,7},{2,0},{3,1},{4,2},{5,3},{6,4},{7,5},{8,14},{9,15},{10,... | collective-permute-start | bytes 98312 | tf_op jit(solution)/shard_map/ppermute | solution.py:278
  134.2 3.0 %collective-permute-start.8 = (f32[8,1024]{1,0:T(8,128)S(1)}, f32[8,1024]{1,0:T(8,128)S(1)}, u32[]{:S(2)}, u32[]{:S(2)}) collective-permute-start(f32[8,1024]{1,0:T(8,128)S(1)} %get-tuple-element.21), channel_id=1, source_target_pairs={{0,4},{1,5},{2,6},{3,7},{4,0},{5,1},{6,2},{7,3},{8,12},{9,13},{10,... | collective-permute-start | bytes 98312 | tf_op jit(solution)/shard_map/ppermute | solution.py:278
  137.3 0.0 all-to-all-done
  137.3 0.0 collective-permute-done.7
  137.3 1.4 collective-permute-done.9
  138.7 1.4 collective-permute-done.8
  140.2 0.1 reshape.38
  140.3 0.7 reshape.39
  (6 shorter events, 0.1 us)
Async XLA Ops:
  6.5 104.3 %reduce-scatter.2.cloned.1.call-start = ((), (), s32[]{:S(2)}) async-start(), calls=%async_computation.2 | async-start | bytes 3407872 | tf_op jit(solution)/shard_map/reduce_scatter | solution.py:235
  43.0 48.8 %copy-start = (s32[1,1,256]{2,1,0:T(1,128)S(1)}, s32[1,1,256]{2,1,0:T(1,128)}, u32[]{:S(2)}) copy-start(s32[1,1,256]{2,1,0:T(1,128)} %param.8) | copy-start | bytes 3076
  43.0 59.1 %copy-start.1 = (s32[1,1,256]{2,1,0:T(1,128)S(1)}, s32[1,1,256]{2,1,0:T(1,128)}, u32[]{:S(2)}) copy-start(s32[1,1,256]{2,1,0:T(1,128)} %param.7) | copy-start | bytes 3076
  71.5 12.9 %collective-permute-start.3 = (f32[96,1024]{1,0:T(8,128)S(1)}, f32[96,1024]{1,0:T(8,128)S(1)}, u32[]{:S(2)}, u32[]{:S(2)}) collective-permute-start(f32[96,1024]{1,0:T(8,128)S(1)} %get-tuple-element.17), channel_id=1, source_target_pairs={{0,48},{8,56},{16,0},{24,8},{32,16},{40,24},{48,32},{56,40},{64,11... | collective-permute-start | bytes 1179656 | tf_op jit(solution)/shard_map/ppermute | solution.py:248
  75.9 11.8 %collective-permute-start = (f32[96,1024]{1,0:T(8,128)S(1)}, f32[96,1024]{1,0:T(8,128)S(1)}, u32[]{:S(2)}, u32[]{:S(2)}) collective-permute-start(f32[96,1024]{1,0:T(8,128)S(1)} %get-tuple-element.18), channel_id=1, source_target_pairs={{0,16},{8,24},{16,32},{24,40},{32,48},{40,56},{48,0},{56,8},{64,80... | collective-permute-start | bytes 1179656 | tf_op jit(solution)/shard_map/ppermute | solution.py:247
  77.8 13.5 %collective-permute-start.1 = (f32[96,1024]{1,0:T(8,128)S(1)}, f32[96,1024]{1,0:T(8,128)S(1)}, u32[]{:S(2)}, u32[]{:S(2)}) collective-permute-start(f32[96,1024]{1,0:T(8,128)S(1)} %get-tuple-element.17), channel_id=1, source_target_pairs={{0,16},{8,24},{16,32},{24,40},{32,48},{40,56},{48,0},{56,8},{64,80... | collective-permute-start | bytes 1179656 | tf_op jit(solution)/shard_map/ppermute | solution.py:249
  79.9 11.9 %collective-permute-start.2 = (f32[96,1024]{1,0:T(8,128)S(1)}, f32[96,1024]{1,0:T(8,128)S(1)}, u32[]{:S(2)}, u32[]{:S(2)}) collective-permute-start(f32[96,1024]{1,0:T(8,128)S(1)} %get-tuple-element.18), channel_id=1, source_target_pairs={{0,48},{8,56},{16,0},{24,8},{32,16},{40,24},{48,32},{56,40},{64,11... | collective-permute-start | bytes 1179656 | tf_op jit(solution)/shard_map/ppermute | solution.py:250
  84.3 15.2 %collective-permute-start.5 = (f32[96,1024]{1,0:T(8,128)S(1)}, f32[96,1024]{1,0:T(8,128)S(1)}, u32[]{:S(2)}, u32[]{:S(2)}) collective-permute-start(f32[96,1024]{1,0:T(8,128)S(1)} %collective-permute-done.3.refs_4_), channel_id=1, source_target_pairs={{0,48},{8,56},{16,0},{24,8},{32,16},{40,24},{48,32},{56,40},{64,11... | collective-permute-start | bytes 1179656 | tf_op jit(solution)/shard_map/ppermute | solution.py:252
  87.7 14.4 %collective-permute-start.4 = (f32[96,1024]{1,0:T(8,128)S(1)}, f32[96,1024]{1,0:T(8,128)S(1)}, u32[]{:S(2)}, u32[]{:S(2)}) collective-permute-start(f32[96,1024]{1,0:T(8,128)S(1)} %collective-permute-done.refs_1_), channel_id=1, source_target_pairs={{0,16},{8,24},{16,32},{24,40},{32,48},{40,56},{48,0},{56,8},{64,80... | collective-permute-start | bytes 1179656 | tf_op jit(solution)/shard_map/ppermute | solution.py:251
  110.9 26.4 %all-to-all-start = ((f32[8,8,1024]{2,1,0:T(8,128)}), f32[8,8,1024]{2,1,0:T(8,128)S(1)}, u32[]{:S(2)}, u32[]{:S(2)}) async-start(f32[8,8,1024]{2,1,0:T(8,128)} %bitcast.19), calls=%async_computation.1 | async-start | bytes 524288 | tf_op jit(solution)/shard_map/all_to_all | solution.py:271
  118.2 8.9 %collective-permute-start.6 = (f32[32,1024]{1,0:T(8,128)S(1)}, f32[32,1024]{1,0:T(8,128)S(1)}, u32[]{:S(2)}, u32[]{:S(2)}) collective-permute-start(f32[32,1024]{1,0:T(8,128)S(1)} %get-tuple-element.16), channel_id=1, source_target_pairs={{0,1},{1,0},{2,3},{3,2},{4,5},{5,4},{6,7},{7,6},{8,9},{9,8},{10,11... | collective-permute-start | bytes 393224 | tf_op jit(solution)/shard_map/ppermute | solution.py:274
  127.2 10.1 %collective-permute-start.7 = (f32[8,1024]{1,0:T(8,128)S(1)}, f32[8,1024]{1,0:T(8,128)S(1)}, u32[]{:S(2)}, u32[]{:S(2)}) collective-permute-start(f32[8,1024]{1,0:T(8,128)S(1)} %get-tuple-element.19), channel_id=1, source_target_pairs={{0,2},{1,3},{2,4},{3,5},{4,6},{5,7},{6,0},{7,1},{8,10},{9,11},{10,... | collective-permute-start | bytes 98312 | tf_op jit(solution)/shard_map/ppermute | solution.py:278
  132.3 6.5 %collective-permute-start.9 = (f32[8,1024]{1,0:T(8,128)S(1)}, f32[8,1024]{1,0:T(8,128)S(1)}, u32[]{:S(2)}, u32[]{:S(2)}) collective-permute-start(f32[8,1024]{1,0:T(8,128)S(1)} %get-tuple-element.20), channel_id=1, source_target_pairs={{0,6},{1,7},{2,0},{3,1},{4,2},{5,3},{6,4},{7,5},{8,14},{9,15},{10,... | collective-permute-start | bytes 98312 | tf_op jit(solution)/shard_map/ppermute | solution.py:278
  134.2 5.9 %collective-permute-start.8 = (f32[8,1024]{1,0:T(8,128)S(1)}, f32[8,1024]{1,0:T(8,128)S(1)}, u32[]{:S(2)}, u32[]{:S(2)}) collective-permute-start(f32[8,1024]{1,0:T(8,128)S(1)} %get-tuple-element.21), channel_id=1, source_target_pairs={{0,4},{1,5},{2,6},{3,7},{4,0},{5,1},{6,2},{7,3},{8,12},{9,13},{10,... | collective-permute-start | bytes 98312 | tf_op jit(solution)/shard_map/ppermute | solution.py:278
Sparse Core Ops, SparseCore 0:
  43.2 58.9 reduce-scatter.1
